TPU v7x, 256 devices: a whole 4x4x8 slice. The times are simulated.
256 devices in a mesh: seq: 32 (over z, x_hi, core), head: 8 (over x_lo, y).
Axes of the slice: x: 4 (x_hi: 2, x_lo: 2; x = x_hi * 2 + x_lo), y: 4, z: 8, core: 2. Of those that a mesh axis runs over, the one named last changes fastest.
Arguments:
- q_one: bfloat16 [4096, 2048], P('seq', 'head'), may hold values from -6 to 6
- q_two: bfloat16 [4096, 2048], P('seq', 'head'), may hold values from -6 to 6
- k_one: bfloat16 [4096, 2048], P('seq', 'head'), may hold values from -6 to 6
- k_two: bfloat16 [4096, 2048], P('seq', 'head'), may hold values from -6 to 6
- values: bfloat16 [4096, 4096], P('seq', 'head'), may hold values from -6 to 6
- out_grad: bfloat16 [4096, 4096], P('seq', 'head'), may hold values from -6 to 6
- lse_one: float32 [16, 4096], P('head', 'seq'), may hold values from 4 to 7
- lse_two: float32 [16, 4096], P('head', 'seq'), may hold values from 4 to 7
- delta_one: float32 [16, 4096], P('head', 'seq'), may hold values from -3 to 3
- delta_two: float32 [16, 4096], P('head', 'seq'), may hold values from -3 to 3
- doc_start: int32 [4096], replicated, may hold values from 0 to 4095, as said below
- skip_pairs: int32 [32, 32], replicated, may hold values from 0 to 1, as said below
- lambda_q1: float32 [128], replicated, may hold values from -0.5 to 0.5
- lambda_k1: float32 [128], replicated, may hold values from -0.5 to 0.5
- lambda_q2: float32 [128], replicated, may hold values from -0.5 to 0.5
- lambda_k2: float32 [128], replicated, may hold values from -0.5 to 0.5
Outputs:
- dq_one: bfloat16 [4096, 2048], P('seq', 'head')
- dq_two: bfloat16 [4096, 2048], P('seq', 'head')
- dk_one: bfloat16 [4096, 2048], P('seq', 'head')
- dk_two: bfloat16 [4096, 2048], P('seq', 'head')
- dv_out: bfloat16 [4096, 4096], P('seq', 'head')
- lambda_grads: float32 [4, 128], replicated
Inputs may be any that keep to these rules, and one draw needn't show every extreme that they name: doc_start of a row is the position of the first token of its document: never above the row's own position, equal for all rows of one document; at position 0 it is 0, and the last position of the sequence starts a document of its own. skip_pairs[s, d] is 1 exactly when no query row held by seq index (d - s) mod the seq size sees any key row held by seq index d under the document and causal rule; row s = 0 is all zero.
All inputs are finite; a program needn't handle non-finite values.
Results may differ from a plain program's by a relative error of at most 0.0072.
Values may be sent and summed in bfloat16 or wider, within the bound.
A program may use at most 64 MiB of HBM per device.

v0:
```python
import math

import jax
import jax.numpy as jnp
from jax import lax
from jax.experimental import pallas as pl
from jax.experimental.pallas import tpu as pltpu
from jax.sharding import PartitionSpec as P

MESH = pl.DeviceIdType.MESH
LAMBDA_INIT = 0.8 - 0.6 * math.exp(-3.6)
F32 = jnp.float32
BF16 = jnp.bfloat16

DK = 128
DV = 256
HALF = 64
COLS = 2 * DK + DV
PLANE = 4
PLANES = 8
DEVICES = PLANE * PLANES
HEAD_DEVICES = 8
LAST = PLANES - 1
FAR = 8192


def nt_dot(a, b):
    return lax.dot_general(a, b, (((1,), (1,)), ((), ())), preferred_element_type=F32)


def tn_dot(a, b):
    return lax.dot_general(a, b, (((0,), (0,)), ((), ())), preferred_element_type=F32)


def nn_dot(a, b):
    return lax.dot_general(a, b, (((1,), (0,)), ((), ())), preferred_element_type=F32)


def kernel(
    q1_ref, q2_ref, go_ref, k1_ref, k2_ref, v_ref,
    lse1_ref, lse2_ref, del1_ref, del2_ref, starts_ref, skip_ref,
    lq1_ref, lk1_ref, lq2_ref, lk2_ref,
    dq1_out, dq2_out, dk1_out, dk2_out, dv_out, lam_out,
    qpay, spay, kpay, kbuf, qbuf, sbuf,
    dqp, dqs, dqr, loc_send, loc_recv, loc_own, fin,
    dkv, dkv_send, dkv_recv,
    lam_acc, lam_send, lam_z, lam_p, lam_h,
    q_send, q_recv, s_send, s_recv, q0_sem, s0_sem, k_send, k_recv,
    d_send, d_recv, f_send, f_recv, l_send, l_recv, o_send, o_recv,
    z_send, z_recv, p_send, p_recv, h_send, h_recv,
):
    me = lax.axis_index("seq")
    hme = lax.axis_index("head")
    z = me // PLANE
    t_me = lax.rem(me, PLANE)
    col = t_me // 2
    core = lax.rem(t_me, 2)
    other = 1 - core
    zdn = lax.rem(z + PLANES - 1, PLANES)
    zup = lax.rem(z + 1, PLANES)

    def dev(zz, cc, kk):
        return zz * PLANE + cc * 2 + kk

    peers = [dev(z, col, other), dev(z, 1 - col, core), dev(z, 1 - col, other)]
    peer_head = [other, core, other]
    peer_t = [2 * col + other, 2 * (1 - col) + core, 2 * (1 - col) + other]
    ring = [zdn, zup]

    def send(src, dst, s_sem, r_sem, seq):
        return pltpu.make_async_remote_copy(
            src_ref=src, dst_ref=dst, send_sem=s_sem, recv_sem=r_sem,
            device_id={"seq": seq}, device_id_type=MESH,
        )

    barrier = pltpu.get_barrier_semaphore()
    for p in peers:
        pl.semaphore_signal(barrier, inc=1, device_id={"seq": p}, device_id_type=MESH)
    for off in range(1, PLANES):
        zz = lax.rem(z + off, PLANES)
        pl.semaphore_signal(barrier, inc=1, device_id={"seq": dev(zz, col, core)}, device_id_type=MESH)
    for zz in ring:
        pl.semaphore_signal(barrier, inc=1, device_id={"seq": dev(zz, col, other)}, device_id_type=MESH)
    for off in range(1, HEAD_DEVICES):
        pl.semaphore_signal(
            barrier, inc=1, device_id={"head": lax.rem(hme + off, HEAD_DEVICES)}, device_id_type=MESH
        )

    for h in range(2):
        for half in range(2):
            rows = slice(half * HALF, (half + 1) * HALF)
            for pay, a, b, g in ((qpay, q1_ref, q2_ref, go_ref), (kpay, k1_ref, k2_ref, v_ref)):
                pay[h, half, :, 0:DK] = a[rows, h * DK:(h + 1) * DK]
                pay[h, half, :, DK:2 * DK] = b[rows, h * DK:(h + 1) * DK]
                pay[h, half, :, 2 * DK:COLS] = g[rows, h * DV:(h + 1) * DV]
        for i, ref in enumerate((lse1_ref, lse2_ref, del1_ref, del2_ref)):
            spay[h, i:i + 1, :] = ref[h:h + 1, :]
        spay[h, 4:8, :] = jnp.zeros((4, 128), F32)

    my_rows = pl.ds(pl.multiple_of(core * HALF, HALF), HALF)
    qbuf[0, :, my_rows, :] = qpay[core]
    sbuf[0, 0, core] = spay[core]
    kbuf[:, t_me] = kpay[core]

    pl.semaphore_wait(barrier, 3 + LAST + 2 + HEAD_DEVICES - 1)

    def first_copies():
        out = []
        for d in range(2):
            for i, (h, k) in enumerate(((core, core), (other, other))):
                to = dev(ring[d], col, k)
                out.append(send(qpay.at[h, d], qbuf.at[1, d, my_rows, :], q_send.at[0, d, i], q_recv.at[1, d], to))
                out.append(send(spay.at[h], sbuf.at[1, d, core], s_send.at[0, d, i], s_recv.at[1, d], to))
        return out

    def key_copies():
        return [
            send(kpay.at[peer_head[i]], kbuf.at[:, t_me], k_send.at[i], k_recv.at[i], peers[i]) for i in range(3)
        ]

    def pair_copies():
        return [
            send(qpay.at[other], qbuf.at[0, :, my_rows, :], q0_sem.at[0], q0_sem.at[1], peers[0]),
            send(spay.at[other], sbuf.at[0, 0, core], s0_sem.at[0], s0_sem.at[1], peers[0]),
        ]

    for cp in first_copies():
        cp.start()
    for cp in key_copies():
        cp.start()
    for cp in pair_copies():
        cp.start()

    e1 = jnp.exp(jnp.sum(lq1_ref[...] * lk1_ref[...], axis=1, keepdims=True))
    e2 = jnp.exp(jnp.sum(lq2_ref[...] * lk2_ref[...], axis=1, keepdims=True))
    mixing = e1 - e2 + LAMBDA_INIT
    scale = DK ** -0.5

    dkv[...] = jnp.zeros_like(dkv)
    lam_acc[...] = jnp.zeros_like(lam_acc)

    def hop_copies(j, d):
        to = dev(ring[d], col, core)
        return (
            send(qbuf.at[j, d], qbuf.at[j + 1, d], q_send.at[j, d, 0], q_recv.at[j + 1, d], to),
            send(sbuf.at[j, d], sbuf.at[j + 1, d], s_send.at[j, d, 0], s_recv.at[j + 1, d], to),
        )

    def dq_copy(j, d):
        return send(dqs.at[j, d], dqr.at[j + 1, d], d_send.at[j, d], d_recv.at[j + 1, d], dev(ring[d], col, core))

    def low_here(j):
        return z + j <= LAST

    def wait_block(j, d):
        pltpu.make_async_copy(qbuf.at[j, d], qbuf.at[j, d], q_recv.at[j, d]).wait()
        pltpu.make_async_copy(sbuf.at[j, d], sbuf.at[j, d], s_recv.at[j, d]).wait()

    lane = lax.broadcasted_iota(jnp.int32, (1, 2 * HALF), 1)
    first = lane < HALF
    sub = lax.broadcasted_iota(jnp.int32, (HALF, 1), 0)

    def merge(a, b, d):
        if d == 0:
            return jnp.where(first, a, pltpu.roll(b, HALF, 1))
        return jnp.where(first, pltpu.roll(a, HALF, 1), b)

    def tile(j, sd, d, zq, kh):
        stats = merge(sbuf[j, sd, 0], sbuf[j, sd, 1], d)
        lse_a, lse_b, del_a, del_b = (stats[i:i + 1] for i in range(4))
        host = PLANE * zq + 2 * col
        starts = merge(starts_ref[pl.ds(host, 1), :], starts_ref[pl.ds(host + 1, 1), :], d)
        if d == 0:
            qpos = host * HALF + lane
        else:
            qpos = jnp.where(first, (2 * DEVICES - 1 - host) * HALF + lane, (2 * DEVICES - 3 - host) * HALF + lane)
        seen = []
        for t in range(PLANE):
            khost = PLANE * z + t
            base = khost * HALF if kh == 0 else (2 * DEVICES - 1 - khost) * HALF
            skip_a = skip_ref[lax.rem(khost - host + DEVICES, DEVICES), khost]
            skip_b = skip_ref[lax.rem(khost - host - 1 + DEVICES, DEVICES), khost]
            start = starts - base + jnp.where(first, skip_a, skip_b) * FAR
            seen.append((sub >= start) & (sub <= qpos - base))
        visible = jnp.concatenate(seen, axis=0)
        qa = qbuf[j, d, :, 0:DK]
        qb = qbuf[j, d, :, DK:2 * DK]
        g = qbuf[j, d, :, 2 * DK:COLS]
        keys = kbuf[kh].reshape(PLANE * HALF, COLS)
        ka, kb, vals = keys[:, 0:DK], keys[:, DK:2 * DK], keys[:, 2 * DK:COLS]
        pa = jnp.where(visible, jnp.exp(nt_dot(ka, qa) * scale - lse_a), 0.0)
        pb = jnp.where(visible, jnp.exp(nt_dot(kb, qb) * scale - lse_b), 0.0)
        inner = nt_dot(vals, g)
        dsa = (pa * (inner - del_a)).astype(BF16)
        dsb = (pb * (-mixing * inner - del_b)).astype(BF16)
        mix = (pa - mixing * pb).astype(BF16)
        lam_acc[...] += jnp.sum((pb * inner).reshape(PLANE * HALF // 8, 8, 2 * HALF), axis=0)
        dkv[kh, :, 0:DK] += nn_dot(dsa, qa)
        dkv[kh, :, DK:2 * DK] += nn_dot(dsb, qb)
        dkv[kh, :, 2 * DK:COLS] += nn_dot(mix, g)
        dqp[d, :, 0:DK] += tn_dot(dsa, ka) * scale
        dqp[d, :, DK:2 * DK] += tn_dot(dsb, kb) * scale

    def home_copies(half):
        return [
            send(
                dkv_send.at[i, half], dkv_recv.at[i, half], o_send.at[i, half], o_recv.at[i, half], peers[i],
            )
            for i in range(3)
        ]

    def send_home(half):
        for i in range(3):
            rows = pl.ds(pl.multiple_of(peer_t[i] * HALF, HALF), HALF)
            dkv_send[i, half, :, 0:2 * DK] = (dkv[half, rows, 0:2 * DK] * scale).astype(BF16)
            dkv_send[i, half, :, 2 * DK:COLS] = dkv[half, rows, 2 * DK:COLS].astype(BF16)
        for cp in home_copies(half):
            cp.start()

    def work(j, d):
        dqp[d] = jnp.zeros((2 * HALF, 2 * DK), F32)
        if d == 0:
            @pl.when(low_here(j))
            def _():
                tile(j, 0, 0, z + j, 0)
        else:
            zq = lax.rem(z - j + PLANES, PLANES)
            tile(j, 1, 1, zq, 0)

            @pl.when(j <= z)
            def _():
                tile(j, 1, 1, zq, 1)

    def take_block(j):
        @pl.when(low_here(j))
        def _():
            wait_block(j, 0)

        wait_block(j, 1)

    def forward(j):
        @pl.when(low_here(j) & (z > 0))
        def _():
            for cp in hop_copies(j, 0):
                cp.start()

        for cp in hop_copies(j, 1):
            cp.start()

    wait_block(1, 0)
    wait_block(1, 1)
    forward(1)

    for cp in pair_copies():
        cp.wait()
    for cp in key_copies():
        cp.wait()
    for d in range(2):
        dqp[d] = jnp.zeros((2 * HALF, 2 * DK), F32)
    tile(0, 0, 0, z, 0)
    tile(0, 0, 1, z, 0)
    tile(0, 0, 1, z, 1)
    their_rows = pl.ds(pl.multiple_of(other * HALF, HALF), HALF)
    for d in range(2):
        loc_own[d] = dqp[d, my_rows, :]
        loc_send[d] = dqp[d, their_rows, :]
    loc_copy = send(loc_send, loc_recv, l_send, l_recv, peers[0])
    loc_copy.start()

    @pl.when(z == 0)
    def _():
        send_home(1)

    take_block(2)
    forward(2)
    for d in range(2):
        work(1, d)
        dqs[1, d] = dqp[d].astype(BF16)
        dq_copy(1, d).start()

    @pl.when(z == 1)
    def _():
        send_home(1)

    def step(j, carry):
        take_block(j + 1)

        @pl.when(j + 1 < LAST)
        def _():
            forward(j + 1)

        for d in range(2):
            work(j, d)
            pltpu.make_async_copy(dqr.at[j, d], dqr.at[j, d], d_recv.at[j, d]).wait()
            dqs[j, d] = (dqr[j, d].astype(F32) + dqp[d]).astype(BF16)
            dq_copy(j, d).start()

        @pl.when(j == z)
        def _():
            send_home(1)

        return carry

    lax.fori_loop(2, LAST, step, 0)

    def fin_copies(d):
        out = []
        for i, k in enumerate((core, other)):
            rows = pl.ds(pl.multiple_of(k * HALF, HALF), HALF)
            out.append(
                send(dqs.at[LAST, d, rows, :], fin.at[d, core], f_send.at[d, i], f_recv.at[d, i], dev(ring[d], col, k))
            )
        return out

    for d in range(2):
        work(LAST, d)
        pltpu.make_async_copy(dqr.at[LAST, d], dqr.at[LAST, d], d_recv.at[LAST, d]).wait()
        dqs[LAST, d] = (dqr[LAST, d].astype(F32) + dqp[d]).astype(BF16)
        for cp in fin_copies(d):
            cp.start()

    @pl.when(z == LAST)
    def _():
        send_home(1)

    send_home(0)

    lam_send[0] = lam_acc[...]
    z_copies = [
        send(lam_send.at[0], lam_z.at[off - 1], z_send.at[off - 1], z_recv.at[off - 1],
             dev(lax.rem(z + off, PLANES), col, core))
        for off in range(1, PLANES)
    ]
    for cp in z_copies:
        cp.start()
    for cp in z_copies:
        cp.wait()
    lam_send[1] = lam_send[0] + jnp.sum(lam_z[...], axis=0)
    p_copies = [send(lam_send.at[1], lam_p.at[i], p_send.at[i], p_recv.at[i], peers[i]) for i in range(3)]
    for cp in p_copies:
        cp.start()
    for cp in p_copies:
        cp.wait()
    lam_send[2] = lam_send[1] + jnp.sum(lam_p[...], axis=0)
    h_copies = [
        pltpu.make_async_remote_copy(
            src_ref=lam_send.at[2], dst_ref=lam_h.at[off - 1], send_sem=h_send.at[off - 1], recv_sem=h_recv.at[off - 1],
            device_id={"head": lax.rem(hme + off, HEAD_DEVICES)}, device_id_type=MESH,
        )
        for off in range(1, HEAD_DEVICES)
    ]
    for cp in h_copies:
        cp.start()

    loc_copy.wait()
    for d in range(2):
        for cp in fin_copies(d):
            cp.wait()
        rows = slice(d * HALF, (d + 1) * HALF)
        mine = loc_own[d] + fin[d, core].astype(F32)
        theirs = loc_recv[d] + fin[d, other].astype(F32)
        for h in range(2):
            val = jnp.where(core == h, mine, theirs).astype(BF16)
            dq1_out[rows, h * DK:(h + 1) * DK] = val[:, 0:DK]
            dq2_out[rows, h * DK:(h + 1) * DK] = val[:, DK:2 * DK]

    key_rows = pl.ds(pl.multiple_of(t_me * HALF, HALF), HALF)
    for half in (1, 0):
        for cp in home_copies(half):
            cp.wait()
        rows = slice(half * HALF, (half + 1) * HALF)
        own = dkv[half, key_rows, :]
        mine_k = own[:, 0:2 * DK] * scale + dkv_recv[1, half, :, 0:2 * DK].astype(F32)
        mine_v = own[:, 2 * DK:COLS] + dkv_recv[1, half, :, 2 * DK:COLS].astype(F32)
        theirs = dkv_recv[0, half].astype(F32) + dkv_recv[2, half].astype(F32)
        for h in range(2):
            val_k = jnp.where(core == h, mine_k, theirs[:, 0:2 * DK]).astype(BF16)
            val_v = jnp.where(core == h, mine_v, theirs[:, 2 * DK:COLS]).astype(BF16)
            dk1_out[rows, h * DK:(h + 1) * DK] = val_k[:, 0:DK]
            dk2_out[rows, h * DK:(h + 1) * DK] = val_k[:, DK:2 * DK]
            dv_out[rows, h * DV:(h + 1) * DV] = val_v

    for cp in h_copies:
        cp.wait()
    total_tile = lam_send[2] + jnp.sum(lam_h[...], axis=0)
    total = -jnp.sum(jnp.sum(total_tile, axis=0, keepdims=True), axis=1, keepdims=True)
    lam_out[0:1, :] = total * e1 * lk1_ref[...]
    lam_out[1:2, :] = total * e1 * lq1_ref[...]
    lam_out[2:3, :] = -total * e2 * lk2_ref[...]
    lam_out[3:4, :] = -total * e2 * lq2_ref[...]

    for cp in first_copies():
        cp.wait_send()
    for j in range(1, LAST):
        @pl.when(low_here(j) & (z > 0))
        def _():
            for cp in hop_copies(j, 0):
                cp.wait_send()

        for cp in hop_copies(j, 1):
            cp.wait_send()
        for d in range(2):
            dq_copy(j, d).wait_send()


def fused(*args):
    (q1, q2, k1, k2, v, go, lse1, lse2, d1, d2, starts, skip, lq1, lk1, lq2, lk2) = args
    rows = q1.shape[0]
    vm = pl.BlockSpec(memory_space=pltpu.VMEM)
    dma = pltpu.SemaphoreType.DMA
    lam_tile = (8, 2 * HALF)
    scratch = [
        pltpu.VMEM((2, 2, HALF, COLS), BF16),
        pltpu.VMEM((2, 8, 2 * HALF), F32),
        pltpu.VMEM((2, 2, HALF, COLS), BF16),
        pltpu.VMEM((2, PLANE, HALF, COLS), BF16),
        pltpu.VMEM((PLANES, 2, 2 * HALF, COLS), BF16),
        pltpu.VMEM((PLANES, 2, 2, 8, 2 * HALF), F32),
        pltpu.VMEM((2, 2 * HALF, 2 * DK), F32),
        pltpu.VMEM((PLANES, 2, 2 * HALF, 2 * DK), BF16),
        pltpu.VMEM((PLANES, 2, 2 * HALF, 2 * DK), BF16),
        pltpu.VMEM((2, HALF, 2 * DK), F32),
        pltpu.VMEM((2, HALF, 2 * DK), F32),
        pltpu.VMEM((2, HALF, 2 * DK), F32),
        pltpu.VMEM((2, 2, HALF, 2 * DK), BF16),
        pltpu.VMEM((2, PLANE * HALF, COLS), F32),
        pltpu.VMEM((3, 2, HALF, COLS), BF16),
        pltpu.VMEM((3, 2, HALF, COLS), BF16),
        pltpu.VMEM(lam_tile, F32),
        pltpu.VMEM((3,) + lam_tile, F32),
        pltpu.VMEM((LAST,) + lam_tile, F32),
        pltpu.VMEM((3,) + lam_tile, F32),
        pltpu.VMEM((HEAD_DEVICES - 1,) + lam_tile, F32),
        dma((PLANES, 2, 2)), dma((PLANES, 2)),
        dma((PLANES, 2, 2)), dma((PLANES, 2)),
        dma((2,)), dma((2,)),
        dma((3,)), dma((3,)),
        dma((PLANES, 2)), dma((PLANES, 2)),
        dma((2, 2)), dma((2, 2)),
        dma, dma,
        dma((3, 2)), dma((3, 2)),
        dma((LAST,)), dma((LAST,)),
        dma((3,)), dma((3,)),
        dma((HEAD_DEVICES - 1,)), dma((HEAD_DEVICES - 1,)),
    ]
    outs = [jax.ShapeDtypeStruct(a.shape, BF16) for a in (q1, q2, k1, k2, v)]
    outs.append(jax.ShapeDtypeStruct((4, DK), F32))
    row = lambda a: a.reshape(1, DK)
    return pl.pallas_call(
        kernel,
        out_shape=outs,
        in_specs=[vm] * 11 + [pl.BlockSpec(memory_space=pltpu.SMEM)] + [vm] * 4,
        out_specs=[vm] * 6,
        scratch_shapes=scratch,
        compiler_params=pltpu.CompilerParams(
            collective_id=0, has_side_effects=True, vmem_limit_bytes=32 * 1024 * 1024
        ),
    )(
        q1, q2, go, k1, k2, v, lse1, lse2, d1, d2, starts.reshape(DEVICES, rows), skip,
        row(lq1), row(lk1), row(lq2), row(lk2),
    )


def solution(mesh):
    tok = P("seq", "head")
    stat = P("head", "seq")
    return jax.shard_map(
        fused,
        mesh=mesh,
        in_specs=(tok,) * 6 + (stat,) * 4 + (P(),) * 6,
        out_specs=(tok,) * 5 + (P(),),
        check_vma=False,
    )
```

profile of v0, /device:TPU:1, one launch (start us, length us, event | category | flops | bytes accessed | tf_op | source)
XLA Modules:
  0.0 78.5 jit_solution(8093611516139750635)
XLA Ops:
  0.6 0.0 copy-start.15
  0.6 0.0 copy-start.11
  0.7 0.0 copy-start.13
  0.7 0.0 copy-start.14
  0.7 0.0 copy-start.9
  0.7 0.0 copy-start.10
  0.7 0.0 copy-start.8
  0.7 0.0 copy-start.12
  0.7 0.6 copy-done.15
  1.3 0.0 copy-done.11
  1.3 0.0 copy-done.13
  1.3 0.0 copy-done.14
  1.3 0.0 copy-done.9
  1.4 0.0 copy-done.10
  1.4 0.0 copy-done.8
  1.4 0.0 copy-done.12
  1.4 0.0 copy-start
  1.4 0.9 %copy-done = bf16[128,512]{1,0:T(8,128)(2,1)S(1)} copy-done((bf16[128,512]{1,0:T(8,128)(2,1)S(1)}, bf16[128,512]{1,0:T(8,128)(2,1)}, u32[]{:S(2)}) %copy-start) | copy-done | bytes 131096
  2.3 0.0 copy-start.1
  2.3 0.9 %copy-done.1 = bf16[128,512]{1,0:T(8,128)(2,1)S(1)} copy-done((bf16[128,512]{1,0:T(8,128)(2,1)S(1)}, bf16[128,512]{1,0:T(8,128)(2,1)}, u32[]{:S(2)}) %copy-start.1) | copy-done | bytes 131096
  3.2 0.0 copy-start.2
  3.2 0.8 %copy-done.2 = bf16[128,256]{1,0:T(8,128)(2,1)S(1)} copy-done((bf16[128,256]{1,0:T(8,128)(2,1)S(1)}, bf16[128,256]{1,0:T(8,128)(2,1)}, u32[]{:S(2)}) %copy-start.2) | copy-done | bytes 65560
  4.1 0.0 copy-start.3
  4.1 0.8 %copy-done.3 = bf16[128,256]{1,0:T(8,128)(2,1)S(1)} copy-done((bf16[128,256]{1,0:T(8,128)(2,1)S(1)}, bf16[128,256]{1,0:T(8,128)(2,1)}, u32[]{:S(2)}) %copy-start.3) | copy-done | bytes 65560
  4.9 0.0 copy-start.4
  4.9 0.8 %copy-done.4 = bf16[128,256]{1,0:T(8,128)(2,1)S(1)} copy-done((bf16[128,256]{1,0:T(8,128)(2,1)S(1)}, bf16[128,256]{1,0:T(8,128)(2,1)}, u32[]{:S(2)}) %copy-start.4) | copy-done | bytes 65560
  5.7 0.0 copy-start.5
  5.7 0.8 %copy-done.5 = bf16[128,256]{1,0:T(8,128)(2,1)S(1)} copy-done((bf16[128,256]{1,0:T(8,128)(2,1)S(1)}, bf16[128,256]{1,0:T(8,128)(2,1)}, u32[]{:S(2)}) %copy-start.5) | copy-done | bytes 65560
  6.6 0.0 copy-start.6
  6.6 0.7 copy-done.6
  7.3 0.0 copy-start.7
  7.3 0.7 copy-done.7
  8.0 66.8 %shard_map.199 = (bf16[128,256]{1,0:T(8,128)(2,1)S(1)}, bf16[128,256]{1,0:T(8,128)(2,1)S(1)}, bf16[128,256]{1,0:T(8,128)(2,1)S(1)}, bf16[128,256]{1,0:T(8,128)(2...) custom-call(bf16[128,256]{1,0:T(8,128)(2,1)S(1)} %copy-done.2, bf16[128,256]{1,0:T(8,128)(2,1)S(1)} %copy-done.3, ...), custom_call_target="tpu_custom_call" | custom-call | tf_op jit(solution)/shard_map/pallas_call | solution.py:449
  74.8 0.6 copy.28
  75.4 0.6 copy.29
  76.1 0.6 copy.30
  76.7 0.6 copy.31
  77.3 0.7 copy.32
  78.0 0.6 copy.33
Async XLA Ops:
  0.6 0.7 copy-start.15
  0.6 0.7 copy-start.11
  0.7 0.7 copy-start.13
  0.7 0.7 copy-start.14
  0.7 0.7 copy-start.9
  0.7 0.7 copy-start.10
  0.7 0.7 copy-start.8
  0.7 0.7 copy-start.12
  1.4 0.9 %copy-start = (bf16[128,512]{1,0:T(8,128)(2,1)S(1)}, bf16[128,512]{1,0:T(8,128)(2,1)}, u32[]{:S(2)}) copy-start(bf16[128,512]{1,0:T(8,128)(2,1)} %go_ref.1) | copy-start | bytes 393220
  2.3 0.9 %copy-start.1 = (bf16[128,512]{1,0:T(8,128)(2,1)S(1)}, bf16[128,512]{1,0:T(8,128)(2,1)}, u32[]{:S(2)}) copy-start(bf16[128,512]{1,0:T(8,128)(2,1)} %v_ref.1) | copy-start | bytes 393220
  3.2 0.8 %copy-start.2 = (bf16[128,256]{1,0:T(8,128)(2,1)S(1)}, bf16[128,256]{1,0:T(8,128)(2,1)}, u32[]{:S(2)}) copy-start(bf16[128,256]{1,0:T(8,128)(2,1)} %q1_ref.1) | copy-start | bytes 196612
  4.1 0.8 %copy-start.3 = (bf16[128,256]{1,0:T(8,128)(2,1)S(1)}, bf16[128,256]{1,0:T(8,128)(2,1)}, u32[]{:S(2)}) copy-start(bf16[128,256]{1,0:T(8,128)(2,1)} %q2_ref.1) | copy-start | bytes 196612
  4.9 0.8 %copy-start.4 = (bf16[128,256]{1,0:T(8,128)(2,1)S(1)}, bf16[128,256]{1,0:T(8,128)(2,1)}, u32[]{:S(2)}) copy-start(bf16[128,256]{1,0:T(8,128)(2,1)} %k1_ref.1) | copy-start | bytes 196612
  5.7 0.8 %copy-start.5 = (bf16[128,256]{1,0:T(8,128)(2,1)S(1)}, bf16[128,256]{1,0:T(8,128)(2,1)}, u32[]{:S(2)}) copy-start(bf16[128,256]{1,0:T(8,128)(2,1)} %k2_ref.1) | copy-start | bytes 196612
  6.6 0.7 copy-start.6
  7.3 0.7 copy-start.7
where the time goes:
time: 79 us; the launch traced here: 78.5 us
  Pallas kernels  66.8 us (85%)
  local copies, waits for them, and re-layouts  11.1 us (14%)
    pallas_call x1, Pallas kernels, fused(): pl.pallas_call(kernel, out_shape=outs, in_specs=[vm] * 11 + [pl.BlockSpec...  66.8 us
    unnamed x38, local copies, waits for them, and re-layouts  11.1 us

commit v1 on v0

--- a/solution.py
+++ b/solution.py
@@ -22,6 +22,7 @@
 HEAD_DEVICES = 8
 LAST = PLANES - 1
 FAR = 8192
+VMEM_LIMIT = 60 * 1024 * 1024
 
 
 def nt_dot(a, b):
@@ -45,7 +46,7 @@
     dqp, dqs, dqr, loc_send, loc_recv, loc_own, fin,
     dkv, dkv_send, dkv_recv,
     lam_acc, lam_send, lam_z, lam_p, lam_h,
-    q_send, q_recv, s_send, s_recv, q0_sem, s0_sem, k_send, k_recv,
+    in_sem, q_send, q_recv, s_send, s_recv, q0_sem, s0_sem, k_send, k_recv,
     d_send, d_recv, f_send, f_recv, l_send, l_recv, o_send, o_recv,
     z_send, z_recv, p_send, p_recv, h_send, h_recv,
 ):
@@ -86,21 +87,23 @@
             barrier, inc=1, device_id={"head": lax.rem(hme + off, HEAD_DEVICES)}, device_id_type=MESH
         )
 
+    packs = []
+    for n, (pay, parts) in enumerate(((qpay, (q1_ref, q2_ref, go_ref)), (kpay, (k1_ref, k2_ref, v_ref)))):
+        for h in range(2):
+            for i, (ref, at, width) in enumerate(zip(parts, (0, DK, 2 * DK), (DK, DK, DV))):
+                cp = pltpu.make_async_copy(
+                    ref.at[:, h * width:(h + 1) * width], pay.at[h, :, at:at + width], in_sem.at[n, h, i]
+                )
+                cp.start()
+                packs.append(cp)
     for h in range(2):
-        for half in range(2):
-            rows = slice(half * HALF, (half + 1) * HALF)
-            for pay, a, b, g in ((qpay, q1_ref, q2_ref, go_ref), (kpay, k1_ref, k2_ref, v_ref)):
-                pay[h, half, :, 0:DK] = a[rows, h * DK:(h + 1) * DK]
-                pay[h, half, :, DK:2 * DK] = b[rows, h * DK:(h + 1) * DK]
-                pay[h, half, :, 2 * DK:COLS] = g[rows, h * DV:(h + 1) * DV]
         for i, ref in enumerate((lse1_ref, lse2_ref, del1_ref, del2_ref)):
             spay[h, i:i + 1, :] = ref[h:h + 1, :]
         spay[h, 4:8, :] = jnp.zeros((4, 128), F32)
 
     my_rows = pl.ds(pl.multiple_of(core * HALF, HALF), HALF)
-    qbuf[0, :, my_rows, :] = qpay[core]
-    sbuf[0, 0, core] = spay[core]
-    kbuf[:, t_me] = kpay[core]
+    for cp in packs:
+        cp.wait()
 
     pl.semaphore_wait(barrier, 3 + LAST + 2 + HEAD_DEVICES - 1)
 
@@ -109,27 +112,37 @@
         for d in range(2):
             for i, (h, k) in enumerate(((core, core), (other, other))):
                 to = dev(ring[d], col, k)
-                out.append(send(qpay.at[h, d], qbuf.at[1, d, my_rows, :], q_send.at[0, d, i], q_recv.at[1, d], to))
+                out.append(send(
+                    qpay.at[h, d * HALF:(d + 1) * HALF], qbuf.at[1, d, my_rows, :], q_send.at[0, d, i],
+                    q_recv.at[1, d, core], to))
                 out.append(send(spay.at[h], sbuf.at[1, d, core], s_send.at[0, d, i], s_recv.at[1, d], to))
         return out
 
     def key_copies():
         return [
-            send(kpay.at[peer_head[i]], kbuf.at[:, t_me], k_send.at[i], k_recv.at[i], peers[i]) for i in range(3)
+            send(kpay.at[peer_head[i], half * HALF:(half + 1) * HALF], kbuf.at[half, t_me], k_send.at[i, half],
+                 k_recv.at[i, half], peers[i])
+            for half in range(2) for i in range(3)
         ]
 
     def pair_copies():
         return [
-            send(qpay.at[other], qbuf.at[0, :, my_rows, :], q0_sem.at[0], q0_sem.at[1], peers[0]),
+            send(qpay.at[other, 0:HALF], qbuf.at[0, 0, my_rows, :], q0_sem.at[0], q0_sem.at[1], peers[0]),
+            send(qpay.at[other, HALF:2 * HALF], qbuf.at[0, 1, my_rows, :], q0_sem.at[2], q0_sem.at[3], peers[0]),
             send(spay.at[other], sbuf.at[0, 0, core], s0_sem.at[0], s0_sem.at[1], peers[0]),
         ]
 
+    for cp in key_copies():
+        cp.start()
     for cp in first_copies():
         cp.start()
-    for cp in key_copies():
-        cp.start()
     for cp in pair_copies():
         cp.start()
+
+    sbuf[0, 0, core] = spay[core]
+    for half in range(2):
+        qbuf[0, half, my_rows, :] = qpay[core, half * HALF:(half + 1) * HALF]
+        kbuf[half, t_me] = kpay[core, half * HALF:(half + 1) * HALF]
 
     e1 = jnp.exp(jnp.sum(lq1_ref[...] * lk1_ref[...], axis=1, keepdims=True))
     e2 = jnp.exp(jnp.sum(lq2_ref[...] * lk2_ref[...], axis=1, keepdims=True))
@@ -139,22 +152,28 @@
     dkv[...] = jnp.zeros_like(dkv)
     lam_acc[...] = jnp.zeros_like(lam_acc)
 
-    def hop_copies(j, d):
+    def piece(i):
+        return slice(i * HALF, (i + 1) * HALF)
+
+    def hop_copies(j, d, i):
         to = dev(ring[d], col, core)
-        return (
-            send(qbuf.at[j, d], qbuf.at[j + 1, d], q_send.at[j, d, 0], q_recv.at[j + 1, d], to),
-            send(sbuf.at[j, d], sbuf.at[j + 1, d], s_send.at[j, d, 0], s_recv.at[j + 1, d], to),
-        )
-
-    def dq_copy(j, d):
-        return send(dqs.at[j, d], dqr.at[j + 1, d], d_send.at[j, d], d_recv.at[j + 1, d], dev(ring[d], col, core))
+        out = [send(qbuf.at[j, d, piece(i)], qbuf.at[j + 1, d, piece(i)], q_send.at[j, d, i], q_recv.at[j + 1, d, i], to)]
+        if i == 1:
+            out.append(send(sbuf.at[j, d], sbuf.at[j + 1, d], s_send.at[j, d, 0], s_recv.at[j + 1, d], to))
+        return out
+
+    def dq_copy(j, d, i):
+        return send(dqs.at[j, d, piece(i)], dqr.at[j + 1, d, piece(i)], d_send.at[j, d, i], d_recv.at[j + 1, d, i],
+                    dev(ring[d], col, core))
 
     def low_here(j):
         return z + j <= LAST
 
-    def wait_block(j, d):
-        pltpu.make_async_copy(qbuf.at[j, d], qbuf.at[j, d], q_recv.at[j, d]).wait()
-        pltpu.make_async_copy(sbuf.at[j, d], sbuf.at[j, d], s_recv.at[j, d]).wait()
+    def wait_piece(j, d, i):
+        block = qbuf.at[j, d, piece(i)]
+        pltpu.make_async_copy(block, block, q_recv.at[j, d, i]).wait()
+        if i == 1:
+            pltpu.make_async_copy(sbuf.at[j, d], sbuf.at[j, d], s_recv.at[j, d]).wait()
 
     lane = lax.broadcasted_iota(jnp.int32, (1, 2 * HALF), 1)
     first = lane < HALF
@@ -231,25 +250,43 @@
             def _():
                 tile(j, 1, 1, zq, 1)
 
-    def take_block(j):
+    def relay(j, i, last):
         @pl.when(low_here(j))
         def _():
-            wait_block(j, 0)
-
-        wait_block(j, 1)
-
-    def forward(j):
-        @pl.when(low_here(j) & (z > 0))
-        def _():
-            for cp in hop_copies(j, 0):
-                cp.start()
-
-        for cp in hop_copies(j, 1):
-            cp.start()
-
-    wait_block(1, 0)
-    wait_block(1, 1)
-    forward(1)
+            wait_piece(j, 0, i)
+
+        if last is not True:
+            @pl.when(low_here(j) & (z > 0) & jnp.logical_not(last))
+            def _():
+                for cp in hop_copies(j, 0, i):
+                    cp.start()
+
+        wait_piece(j, 1, i)
+        if last is not True:
+            @pl.when(jnp.logical_not(last))
+            def _():
+                for cp in hop_copies(j, 1, i):
+                    cp.start()
+
+    def pass_sums(j, d, first_hop):
+        for i in range(2):
+            part = dqp[d, piece(i)]
+            if not first_hop:
+                block = dqr.at[j, d, piece(i)]
+                pltpu.make_async_copy(block, block, d_recv.at[j, d, i]).wait()
+                part = part + dqr[j, d, piece(i)].astype(F32)
+            dqs[j, d, piece(i)] = part.astype(BF16)
+            if j is not LAST:
+                dq_copy(j, d, i).start()
+
+    for i in range(2):
+        for d in range(2):
+            wait_piece(1, d, i)
+
+            @pl.when((d == 1) | (low_here(1) & (z > 0)))
+            def _():
+                for cp in hop_copies(1, d, i):
+                    cp.start()
 
     for cp in pair_copies():
         cp.wait()
@@ -271,29 +308,20 @@
     def _():
         send_home(1)
 
-    take_block(2)
-    forward(2)
     for d in range(2):
+        relay(2, d, False)
         work(1, d)
-        dqs[1, d] = dqp[d].astype(BF16)
-        dq_copy(1, d).start()
+        pass_sums(1, d, True)
 
     @pl.when(z == 1)
     def _():
         send_home(1)
 
     def step(j, carry):
-        take_block(j + 1)
-
-        @pl.when(j + 1 < LAST)
-        def _():
-            forward(j + 1)
-
         for d in range(2):
+            relay(j + 1, d, j + 1 == LAST)
             work(j, d)
-            pltpu.make_async_copy(dqr.at[j, d], dqr.at[j, d], d_recv.at[j, d]).wait()
-            dqs[j, d] = (dqr[j, d].astype(F32) + dqp[d]).astype(BF16)
-            dq_copy(j, d).start()
+            pass_sums(j, d, False)
 
         @pl.when(j == z)
         def _():
@@ -314,8 +342,7 @@
 
     for d in range(2):
         work(LAST, d)
-        pltpu.make_async_copy(dqr.at[LAST, d], dqr.at[LAST, d], d_recv.at[LAST, d]).wait()
-        dqs[LAST, d] = (dqr[LAST, d].astype(F32) + dqp[d]).astype(BF16)
+        pass_sums(LAST, d, False)
         for cp in fin_copies(d):
             cp.start()
 
@@ -392,27 +419,38 @@
     for cp in first_copies():
         cp.wait_send()
     for j in range(1, LAST):
-        @pl.when(low_here(j) & (z > 0))
-        def _():
-            for cp in hop_copies(j, 0):
+        for i in range(2):
+            @pl.when(low_here(j) & (z > 0))
+            def _():
+                for cp in hop_copies(j, 0, i):
+                    cp.wait_send()
+
+            for cp in hop_copies(j, 1, i):
                 cp.wait_send()
-
-        for cp in hop_copies(j, 1):
-            cp.wait_send()
-        for d in range(2):
-            dq_copy(j, d).wait_send()
+            for d in range(2):
+                dq_copy(j, d, i).wait_send()
+
+
+def finish(*refs):
+    n = len(refs) // 2
+    copies = [pltpu.make_async_copy(refs[i], refs[n + i], refs[-1].at[i]) for i in range(n)]
+    for cp in copies:
+        cp.start()
+    for cp in copies:
+        cp.wait()
 
 
 def fused(*args):
     (q1, q2, k1, k2, v, go, lse1, lse2, d1, d2, starts, skip, lq1, lk1, lq2, lk2) = args
     rows = q1.shape[0]
     vm = pl.BlockSpec(memory_space=pltpu.VMEM)
+    hbm = pl.BlockSpec(memory_space=pltpu.HBM)
     dma = pltpu.SemaphoreType.DMA
     lam_tile = (8, 2 * HALF)
     scratch = [
-        pltpu.VMEM((2, 2, HALF, COLS), BF16),
+        pltpu.VMEM((2, 2 * HALF, COLS), BF16),
         pltpu.VMEM((2, 8, 2 * HALF), F32),
-        pltpu.VMEM((2, 2, HALF, COLS), BF16),
+        pltpu.VMEM((2, 2 * HALF, COLS), BF16),
         pltpu.VMEM((2, PLANE, HALF, COLS), BF16),
         pltpu.VMEM((PLANES, 2, 2 * HALF, COLS), BF16),
         pltpu.VMEM((PLANES, 2, 2, 8, 2 * HALF), F32),
@@ -431,11 +469,12 @@
         pltpu.VMEM((LAST,) + lam_tile, F32),
         pltpu.VMEM((3,) + lam_tile, F32),
         pltpu.VMEM((HEAD_DEVICES - 1,) + lam_tile, F32),
+        dma((2, 2, 3)),
+        dma((PLANES, 2, 2)), dma((PLANES, 2, 2)),
         dma((PLANES, 2, 2)), dma((PLANES, 2)),
-        dma((PLANES, 2, 2)), dma((PLANES, 2)),
-        dma((2,)), dma((2,)),
-        dma((3,)), dma((3,)),
-        dma((PLANES, 2)), dma((PLANES, 2)),
+        dma((4,)), dma((2,)),
+        dma((3, 2)), dma((3, 2)),
+        dma((PLANES, 2, 2)), dma((PLANES, 2, 2)),
         dma((2, 2)), dma((2, 2)),
         dma, dma,
         dma((3, 2)), dma((3, 2)),
@@ -446,19 +485,27 @@
     outs = [jax.ShapeDtypeStruct(a.shape, BF16) for a in (q1, q2, k1, k2, v)]
     outs.append(jax.ShapeDtypeStruct((4, DK), F32))
     row = lambda a: a.reshape(1, DK)
-    return pl.pallas_call(
+    results = pl.pallas_call(
         kernel,
-        out_shape=outs,
-        in_specs=[vm] * 11 + [pl.BlockSpec(memory_space=pltpu.SMEM)] + [vm] * 4,
+        out_shape=[pltpu.VMEM(o.shape, o.dtype) for o in outs],
+        in_specs=[hbm] * 6 + [vm] * 5 + [pl.BlockSpec(memory_space=pltpu.SMEM)] + [vm] * 4,
         out_specs=[vm] * 6,
         scratch_shapes=scratch,
         compiler_params=pltpu.CompilerParams(
-            collective_id=0, has_side_effects=True, vmem_limit_bytes=32 * 1024 * 1024
+            collective_id=0, has_side_effects=True, vmem_limit_bytes=VMEM_LIMIT
         ),
     )(
         q1, q2, go, k1, k2, v, lse1, lse2, d1, d2, starts.reshape(DEVICES, rows), skip,
         row(lq1), row(lk1), row(lq2), row(lk2),
     )
+    return pl.pallas_call(
+        finish,
+        out_shape=outs,
+        in_specs=[vm] * 6,
+        out_specs=[hbm] * 6,
+        scratch_shapes=[dma((6,))],
+        compiler_params=pltpu.CompilerParams(vmem_limit_bytes=8 * 1024 * 1024),
+    )(*results)
 
 
 def solution(mesh):

time: 79 us -> 65.2 us (0.83)
  local copies, waits for them, and re-layouts: 11.1 us -> 0 us
  Pallas kernels: 66.8 us -> 64.3 us
    unnamed x38 -> x0, local copies, waits for them, and re-layouts: 11.1 us -> none
    pallas_call x1 -> x2, Pallas kernels: 66.8 us -> 64.3 us  [the longest x1 63.5 us: fused(): pl.pallas_call(kernel, out_shape=[pltpu.VMEM(o.shape, o.dtype) for o in o...]
where the time goes in v1:
time: 65.2 us; the launch traced here: 65 us
  Pallas kernels  64.3 us (99%)
    pallas_call x1, Pallas kernels, fused(): pl.pallas_call(kernel, out_shape=[pltpu.VMEM(o.shape, o.dtype) for o in o...  63.5 us

profile of v1, /device:TPU:1, one launch (start us, length us, event | category | flops | bytes accessed | tf_op | source)
XLA Modules:
  0.0 65.0 jit_solution(13195562997838708761)
XLA Ops:
  0.6 63.5 %shard_map.199 = (bf16[128,256]{1,0:T(8,128)(2,1)S(1)}, bf16[128,256]{1,0:T(8,128)(2,1)S(1)}, bf16[128,256]{1,0:T(8,128)(2,1)S(1)}, bf16[128,256]{1,0:T(8,128)(2...) custom-call(bf16[128,256]{1,0:T(8,128)(2,1)} %q1_ref.1, bf16[128,256]{1,0:T(8,128)(2,1)} %q2_ref.1, ...), custom_call_target="tpu_custom_call" | custom-call | tf_op jit(solution)/shard_map/pallas_call | solution.py:488
  64.2 0.8 %shard_map.200 = (bf16[128,256]{1,0:T(8,128)(2,1)}, bf16[128,256]{1,0:T(8,128)(2,1)}, bf16[128,256]{1,0:T(8,128)(2,1)}, bf16[128,256]{1,0:T(8,128)(2,1)}, bf16[128,512]{1,0:T(8,128)(2,1)}, /*index=5*/f32[4,128]{1,0:T(4,128)}) custom-call(bf16[128,256]{1,0:T(8,128)(2,1)S(1)} %get-tuple-element.12.refs_0_, bf16[128,256]{1,0:T(8,128)(2,1)S(1)} %get-tuple-element.13.refs_1_, ...), custom_call_target="tpu_custom_call" | custom-call | tf_op jit(solution)/shard_map/pallas_call | solution.py:501

commit v2 on v1

--- a/solution.py
+++ b/solution.py
@@ -39,16 +39,18 @@
 
 def kernel(
     q1_ref, q2_ref, go_ref, k1_ref, k2_ref, v_ref,
+    lse1_hbm, lse2_hbm, del1_hbm, del2_hbm, starts_hbm, skip_hbm,
+    lq1_hbm, lk1_hbm, lq2_hbm, lk2_hbm,
+    dq1_out, dq2_out, dk1_out, dk2_out, dv_out, lam_out,
     lse1_ref, lse2_ref, del1_ref, del2_ref, starts_ref, skip_ref,
     lq1_ref, lk1_ref, lq2_ref, lk2_ref,
-    dq1_out, dq2_out, dk1_out, dk2_out, dv_out, lam_out,
     qpay, spay, kpay, kbuf, qbuf, sbuf,
-    dqp, dqs, dqr, loc_send, loc_recv, loc_own, fin,
+    dqp, dqs, dqr, loc_send, loc_recv, fin,
     dkv, dkv_send, dkv_recv,
-    lam_acc, lam_send, lam_z, lam_p, lam_h,
-    in_sem, q_send, q_recv, s_send, s_recv, q0_sem, s0_sem, k_send, k_recv,
+    lam_acc, lam_send, lam_x, lam_z, lam_y,
+    in_sem, small_sem, q_send, q_recv, s_send, s_recv, q0_sem, s0_sem, k_send, k_recv,
     d_send, d_recv, f_send, f_recv, l_send, l_recv, o_send, o_recv,
-    z_send, z_recv, p_send, p_recv, h_send, h_recv,
+    x_send, x_recv, z_send, z_recv, y_send, y_recv,
 ):
     me = lax.axis_index("seq")
     hme = lax.axis_index("head")
@@ -74,21 +76,27 @@
             device_id={"seq": seq}, device_id_type=MESH,
         )
 
+    across = lax.rem(hme + HEAD_DEVICES // 2, HEAD_DEVICES)
+    y_me = lax.rem(hme, HEAD_DEVICES // 2)
+    beside = [hme - y_me + lax.rem(y_me + off, HEAD_DEVICES // 2) for off in range(1, HEAD_DEVICES // 2)]
+
     barrier = pltpu.get_barrier_semaphore()
     for p in peers:
         pl.semaphore_signal(barrier, inc=1, device_id={"seq": p}, device_id_type=MESH)
     for off in range(1, PLANES):
         zz = lax.rem(z + off, PLANES)
         pl.semaphore_signal(barrier, inc=1, device_id={"seq": dev(zz, col, core)}, device_id_type=MESH)
-    for zz in ring:
+    for zz in (zdn, zup):
         pl.semaphore_signal(barrier, inc=1, device_id={"seq": dev(zz, col, other)}, device_id_type=MESH)
-    for off in range(1, HEAD_DEVICES):
+    for t in range(PLANE):
         pl.semaphore_signal(
-            barrier, inc=1, device_id={"head": lax.rem(hme + off, HEAD_DEVICES)}, device_id_type=MESH
+            barrier, inc=1, device_id={"seq": z * PLANE + t, "head": across}, device_id_type=MESH
         )
+    for yy in beside:
+        pl.semaphore_signal(barrier, inc=1, device_id={"head": yy}, device_id_type=MESH)
 
     packs = []
-    for n, (pay, parts) in enumerate(((qpay, (q1_ref, q2_ref, go_ref)), (kpay, (k1_ref, k2_ref, v_ref)))):
+    for n, (pay, parts) in enumerate(((kpay, (k1_ref, k2_ref, v_ref)), (qpay, (q1_ref, q2_ref, go_ref)))):
         for h in range(2):
             for i, (ref, at, width) in enumerate(zip(parts, (0, DK, 2 * DK), (DK, DK, DV))):
                 cp = pltpu.make_async_copy(
@@ -96,16 +104,31 @@
                 )
                 cp.start()
                 packs.append(cp)
+    small = [
+        pltpu.make_async_copy(a, b, small_sem.at[i])
+        for i, (a, b) in enumerate((
+            (lse1_hbm, lse1_ref), (lse2_hbm, lse2_ref), (del1_hbm, del1_ref), (del2_hbm, del2_ref),
+            (starts_hbm, starts_ref), (skip_hbm, skip_ref),
+            (lq1_hbm, lq1_ref), (lk1_hbm, lk1_ref), (lq2_hbm, lq2_ref), (lk2_hbm, lk2_ref),
+        ))
+    ]
+    for cp in small:
+        cp.start()
+
+    for cp in small:
+        cp.wait()
     for h in range(2):
         for i, ref in enumerate((lse1_ref, lse2_ref, del1_ref, del2_ref)):
             spay[h, i:i + 1, :] = ref[h:h + 1, :]
         spay[h, 4:8, :] = jnp.zeros((4, 128), F32)
+    dkv[...] = jnp.zeros_like(dkv)
+    lam_acc[...] = jnp.zeros_like(lam_acc)
 
     my_rows = pl.ds(pl.multiple_of(core * HALF, HALF), HALF)
     for cp in packs:
         cp.wait()
 
-    pl.semaphore_wait(barrier, 3 + LAST + 2 + HEAD_DEVICES - 1)
+    pl.semaphore_wait(barrier, 3 + LAST + 2 + PLANE + 3)
 
     def first_copies():
         out = []
@@ -132,12 +155,22 @@
             send(spay.at[other], sbuf.at[0, 0, core], s0_sem.at[0], s0_sem.at[1], peers[0]),
         ]
 
+    @pl.when(core == 0)
+    def _():
+        for cp in first_copies():
+            cp.start()
+
+    for cp in pair_copies():
+        cp.start()
     for cp in key_copies():
         cp.start()
-    for cp in first_copies():
-        cp.start()
     for cp in pair_copies():
-        cp.start()
+        cp.wait()
+
+    @pl.when(core == 1)
+    def _():
+        for cp in first_copies():
+            cp.start()
 
     sbuf[0, 0, core] = spay[core]
     for half in range(2):
@@ -148,9 +181,6 @@
     e2 = jnp.exp(jnp.sum(lq2_ref[...] * lk2_ref[...], axis=1, keepdims=True))
     mixing = e1 - e2 + LAMBDA_INIT
     scale = DK ** -0.5
-
-    dkv[...] = jnp.zeros_like(dkv)
-    lam_acc[...] = jnp.zeros_like(lam_acc)
 
     def piece(i):
         return slice(i * HALF, (i + 1) * HALF)
@@ -217,8 +247,8 @@
         dkv[kh, :, 0:DK] += nn_dot(dsa, qa)
         dkv[kh, :, DK:2 * DK] += nn_dot(dsb, qb)
         dkv[kh, :, 2 * DK:COLS] += nn_dot(mix, g)
-        dqp[d, :, 0:DK] += tn_dot(dsa, ka) * scale
-        dqp[d, :, DK:2 * DK] += tn_dot(dsb, kb) * scale
+        dqp[j, d, :, 0:DK] += tn_dot(dsa, ka) * scale
+        dqp[j, d, :, DK:2 * DK] += tn_dot(dsb, kb) * scale
 
     def home_copies(half):
         return [
@@ -237,7 +267,7 @@
             cp.start()
 
     def work(j, d):
-        dqp[d] = jnp.zeros((2 * HALF, 2 * DK), F32)
+        dqp[j, d] = jnp.zeros((2 * HALF, 2 * DK), F32)
         if d == 0:
             @pl.when(low_here(j))
             def _():
@@ -270,7 +300,7 @@
 
     def pass_sums(j, d, first_hop):
         for i in range(2):
-            part = dqp[d, piece(i)]
+            part = dqp[j, d, piece(i)]
             if not first_hop:
                 block = dqr.at[j, d, piece(i)]
                 pltpu.make_async_copy(block, block, d_recv.at[j, d, i]).wait()
@@ -287,20 +317,19 @@
             def _():
                 for cp in hop_copies(1, d, i):
                     cp.start()
-
-    for cp in pair_copies():
-        cp.wait()
+    for i in range(2):
+        relay(2, i, False)
+
     for cp in key_copies():
         cp.wait()
     for d in range(2):
-        dqp[d] = jnp.zeros((2 * HALF, 2 * DK), F32)
+        dqp[0, d] = jnp.zeros((2 * HALF, 2 * DK), F32)
     tile(0, 0, 0, z, 0)
     tile(0, 0, 1, z, 0)
     tile(0, 0, 1, z, 1)
     their_rows = pl.ds(pl.multiple_of(other * HALF, HALF), HALF)
     for d in range(2):
-        loc_own[d] = dqp[d, my_rows, :]
-        loc_send[d] = dqp[d, their_rows, :]
+        loc_send[d] = dqp[0, d, their_rows, :]
     loc_copy = send(loc_send, loc_recv, l_send, l_recv, peers[0])
     loc_copy.start()
 
@@ -308,20 +337,23 @@
     def _():
         send_home(1)
 
-    for d in range(2):
-        relay(2, d, False)
-        work(1, d)
-        pass_sums(1, d, True)
-
-    @pl.when(z == 1)
-    def _():
-        send_home(1)
-
     def step(j, carry):
+        @pl.when(j > 2)
+        def _():
+            relay(j, 0, j == LAST)
+            relay(j, 1, j == LAST)
+
         for d in range(2):
-            relay(j + 1, d, j + 1 == LAST)
+            @pl.when(j == 2)
+            def _():
+                pass_sums(1, d, True)
+
+            @pl.when(j > 2)
+            def _():
+                pass_sums(j - 1, d, False)
+
+        for d in range(2):
             work(j, d)
-            pass_sums(j, d, False)
 
         @pl.when(j == z)
         def _():
@@ -329,7 +361,7 @@
 
         return carry
 
-    lax.fori_loop(2, LAST, step, 0)
+    lax.fori_loop(1, LAST + 1, step, 0)
 
     def fin_copies(d):
         out = []
@@ -340,56 +372,45 @@
             )
         return out
 
+    x_copies = [send(lam_send.at[0], lam_x.at[i], x_send.at[i], x_recv.at[i], peers[i]) for i in range(3)] + [
+        pltpu.make_async_remote_copy(
+            src_ref=lam_send.at[0], dst_ref=lam_x.at[3 + i], send_sem=x_send.at[3 + i], recv_sem=x_recv.at[3 + i],
+            device_id={"seq": to, "head": across}, device_id_type=MESH,
+        )
+        for i, to in enumerate([me] + peers)
+    ]
+    z_copies = [
+        send(lam_send.at[1], lam_z.at[off - 1], z_send.at[off - 1], z_recv.at[off - 1],
+             dev(lax.rem(z + off, PLANES), col, core))
+        for off in range(1, PLANES)
+    ]
+    y_copies = [
+        pltpu.make_async_remote_copy(
+            src_ref=lam_send.at[2], dst_ref=lam_y.at[i], send_sem=y_send.at[i], recv_sem=y_recv.at[i],
+            device_id={"head": to}, device_id_type=MESH,
+        )
+        for i, to in enumerate(beside)
+    ]
+
+    def lam_stage(n):
+        if n > 0:
+            parts = (x_copies, z_copies)[n - 1]
+            for cp in parts:
+                cp.wait()
+            lam_send[n] = lam_send[n - 1] + jnp.sum((lam_x, lam_z)[n - 1][...], axis=0)
+        else:
+            lam_send[0] = lam_acc[...]
+        for cp in (x_copies, z_copies, y_copies)[n]:
+            cp.start()
+
+    lam_stage(0)
+    send_home(0)
+    lam_stage(1)
     for d in range(2):
-        work(LAST, d)
         pass_sums(LAST, d, False)
         for cp in fin_copies(d):
             cp.start()
-
-    @pl.when(z == LAST)
-    def _():
-        send_home(1)
-
-    send_home(0)
-
-    lam_send[0] = lam_acc[...]
-    z_copies = [
-        send(lam_send.at[0], lam_z.at[off - 1], z_send.at[off - 1], z_recv.at[off - 1],
-             dev(lax.rem(z + off, PLANES), col, core))
-        for off in range(1, PLANES)
-    ]
-    for cp in z_copies:
-        cp.start()
-    for cp in z_copies:
-        cp.wait()
-    lam_send[1] = lam_send[0] + jnp.sum(lam_z[...], axis=0)
-    p_copies = [send(lam_send.at[1], lam_p.at[i], p_send.at[i], p_recv.at[i], peers[i]) for i in range(3)]
-    for cp in p_copies:
-        cp.start()
-    for cp in p_copies:
-        cp.wait()
-    lam_send[2] = lam_send[1] + jnp.sum(lam_p[...], axis=0)
-    h_copies = [
-        pltpu.make_async_remote_copy(
-            src_ref=lam_send.at[2], dst_ref=lam_h.at[off - 1], send_sem=h_send.at[off - 1], recv_sem=h_recv.at[off - 1],
-            device_id={"head": lax.rem(hme + off, HEAD_DEVICES)}, device_id_type=MESH,
-        )
-        for off in range(1, HEAD_DEVICES)
-    ]
-    for cp in h_copies:
-        cp.start()
-
-    loc_copy.wait()
-    for d in range(2):
-        for cp in fin_copies(d):
-            cp.wait()
-        rows = slice(d * HALF, (d + 1) * HALF)
-        mine = loc_own[d] + fin[d, core].astype(F32)
-        theirs = loc_recv[d] + fin[d, other].astype(F32)
-        for h in range(2):
-            val = jnp.where(core == h, mine, theirs).astype(BF16)
-            dq1_out[rows, h * DK:(h + 1) * DK] = val[:, 0:DK]
-            dq2_out[rows, h * DK:(h + 1) * DK] = val[:, DK:2 * DK]
+    lam_stage(2)
 
     key_rows = pl.ds(pl.multiple_of(t_me * HALF, HALF), HALF)
     for half in (1, 0):
@@ -407,9 +428,21 @@
             dk2_out[rows, h * DK:(h + 1) * DK] = val_k[:, DK:2 * DK]
             dv_out[rows, h * DV:(h + 1) * DV] = val_v
 
-    for cp in h_copies:
+    loc_copy.wait()
+    for d in range(2):
+        for cp in fin_copies(d):
+            cp.wait()
+        rows = slice(d * HALF, (d + 1) * HALF)
+        mine = dqp[0, d, my_rows, :] + fin[d, core].astype(F32)
+        theirs = loc_recv[d] + fin[d, other].astype(F32)
+        for h in range(2):
+            val = jnp.where(core == h, mine, theirs).astype(BF16)
+            dq1_out[rows, h * DK:(h + 1) * DK] = val[:, 0:DK]
+            dq2_out[rows, h * DK:(h + 1) * DK] = val[:, DK:2 * DK]
+
+    for cp in y_copies:
         cp.wait()
-    total_tile = lam_send[2] + jnp.sum(lam_h[...], axis=0)
+    total_tile = lam_send[2] + jnp.sum(lam_y[...], axis=0)
     total = -jnp.sum(jnp.sum(total_tile, axis=0, keepdims=True), axis=1, keepdims=True)
     lam_out[0:1, :] = total * e1 * lk1_ref[...]
     lam_out[1:2, :] = total * e1 * lq1_ref[...]
@@ -448,16 +481,19 @@
     dma = pltpu.SemaphoreType.DMA
     lam_tile = (8, 2 * HALF)
     scratch = [
+        *[pltpu.VMEM((2, 2 * HALF), F32)] * 4,
+        pltpu.VMEM((DEVICES, 2 * HALF), jnp.int32),
+        pltpu.SMEM((DEVICES, DEVICES), jnp.int32),
+        *[pltpu.VMEM((1, DK), F32)] * 4,
         pltpu.VMEM((2, 2 * HALF, COLS), BF16),
         pltpu.VMEM((2, 8, 2 * HALF), F32),
         pltpu.VMEM((2, 2 * HALF, COLS), BF16),
         pltpu.VMEM((2, PLANE, HALF, COLS), BF16),
         pltpu.VMEM((PLANES, 2, 2 * HALF, COLS), BF16),
         pltpu.VMEM((PLANES, 2, 2, 8, 2 * HALF), F32),
-        pltpu.VMEM((2, 2 * HALF, 2 * DK), F32),
+        pltpu.VMEM((PLANES, 2, 2 * HALF, 2 * DK), F32),
         pltpu.VMEM((PLANES, 2, 2 * HALF, 2 * DK), BF16),
         pltpu.VMEM((PLANES, 2, 2 * HALF, 2 * DK), BF16),
-        pltpu.VMEM((2, HALF, 2 * DK), F32),
         pltpu.VMEM((2, HALF, 2 * DK), F32),
         pltpu.VMEM((2, HALF, 2 * DK), F32),
         pltpu.VMEM((2, 2, HALF, 2 * DK), BF16),
@@ -467,9 +503,9 @@
         pltpu.VMEM(lam_tile, F32),
         pltpu.VMEM((3,) + lam_tile, F32),
         pltpu.VMEM((LAST,) + lam_tile, F32),
+        pltpu.VMEM((LAST,) + lam_tile, F32),
         pltpu.VMEM((3,) + lam_tile, F32),
-        pltpu.VMEM((HEAD_DEVICES - 1,) + lam_tile, F32),
-        dma((2, 2, 3)),
+        dma((2, 2, 3)), dma((10,)),
         dma((PLANES, 2, 2)), dma((PLANES, 2, 2)),
         dma((PLANES, 2, 2)), dma((PLANES, 2)),
         dma((4,)), dma((2,)),
@@ -479,8 +515,8 @@
         dma, dma,
         dma((3, 2)), dma((3, 2)),
         dma((LAST,)), dma((LAST,)),
+        dma((LAST,)), dma((LAST,)),
         dma((3,)), dma((3,)),
-        dma((HEAD_DEVICES - 1,)), dma((HEAD_DEVICES - 1,)),
     ]
     outs = [jax.ShapeDtypeStruct(a.shape, BF16) for a in (q1, q2, k1, k2, v)]
     outs.append(jax.ShapeDtypeStruct((4, DK), F32))
@@ -488,7 +524,7 @@
     results = pl.pallas_call(
         kernel,
         out_shape=[pltpu.VMEM(o.shape, o.dtype) for o in outs],
-        in_specs=[hbm] * 6 + [vm] * 5 + [pl.BlockSpec(memory_space=pltpu.SMEM)] + [vm] * 4,
+        in_specs=[hbm] * 16,
         out_specs=[vm] * 6,
         scratch_shapes=scratch,
         compiler_params=pltpu.CompilerParams(

time: 65.2 us -> 59.8 us (0.917)
  Pallas kernels: 64.3 us -> 59.1 us
    pallas_call x1, Pallas kernels: 63.5 us -> 58.3 us  [fused(): pl.pallas_call(kernel, out_shape=[pltpu.VMEM(o.shape, o.dtype) for o in o...]
where the time goes in v2:
time: 59.8 us; the launch traced here: 59.7 us
  Pallas kernels  59.1 us (99%)
  between operations  0.65 us (1%)
    pallas_call x1, Pallas kernels, fused(): pl.pallas_call(kernel, out_shape=[pltpu.VMEM(o.shape, o.dtype) for o in o...  58.3 us

profile of v2, /device:TPU:1, one launch (start us, length us, event | category | flops | bytes accessed | tf_op | source)
XLA Modules:
  0.0 59.7 jit_solution(2177377117478211455)
XLA Ops:
  0.6 58.3 %shard_map.199 = (bf16[128,256]{1,0:T(8,128)(2,1)S(1)}, bf16[128,256]{1,0:T(8,128)(2,1)S(1)}, bf16[128,256]{1,0:T(8,128)(2,1)S(1)}, bf16[128,256]{1,0:T(8,128)(2...) custom-call(bf16[128,256]{1,0:T(8,128)(2,1)} %q1_ref.1, bf16[128,256]{1,0:T(8,128)(2,1)} %q2_ref.1, ...), custom_call_target="tpu_custom_call" | custom-call | tf_op jit(solution)/shard_map/pallas_call | solution.py:524
  58.9 0.8 %shard_map.200 = (bf16[128,256]{1,0:T(8,128)(2,1)}, bf16[128,256]{1,0:T(8,128)(2,1)}, bf16[128,256]{1,0:T(8,128)(2,1)}, bf16[128,256]{1,0:T(8,128)(2,1)}, bf16[128,512]{1,0:T(8,128)(2,1)}, /*index=5*/f32[4,128]{1,0:T(4,128)}) custom-call(bf16[128,256]{1,0:T(8,128)(2,1)S(1)} %get-tuple-element.12.refs_0_, bf16[128,256]{1,0:T(8,128)(2,1)S(1)} %get-tuple-element.13.refs_1_, ...), custom_call_target="tpu_custom_call" | custom-call | tf_op jit(solution)/shard_map/pallas_call | solution.py:537

commit v3 on v2

--- a/solution.py
+++ b/solution.py
@@ -320,8 +320,12 @@
     for i in range(2):
         relay(2, i, False)
 
-    for cp in key_copies():
-        cp.wait()
+    for d in range(2):
+        for cp in key_copies()[3 * d:3 * d + 3]:
+            cp.wait()
+        work(1, d)
+        pass_sums(1, d, True)
+
     for d in range(2):
         dqp[0, d] = jnp.zeros((2 * HALF, 2 * DK), F32)
     tile(0, 0, 0, z, 0)
@@ -333,7 +337,7 @@
     loc_copy = send(loc_send, loc_recv, l_send, l_recv, peers[0])
     loc_copy.start()
 
-    @pl.when(z == 0)
+    @pl.when(z <= 1)
     def _():
         send_home(1)
 
@@ -344,10 +348,6 @@
             relay(j, 1, j == LAST)
 
         for d in range(2):
-            @pl.when(j == 2)
-            def _():
-                pass_sums(1, d, True)
-
             @pl.when(j > 2)
             def _():
                 pass_sums(j - 1, d, False)
@@ -361,7 +361,7 @@
 
         return carry
 
-    lax.fori_loop(1, LAST + 1, step, 0)
+    lax.fori_loop(2, LAST + 1, step, 0)
 
     def fin_copies(d):
         out = []

time: 59.8 us -> 59.5 us (level)
  no operation moved by 1% of the time
where the time goes in v3:
time: 59.5 us; the launch traced here: 59.3 us
  Pallas kernels  58.7 us (99%)
  between operations  0.65 us (1%)
    pallas_call x1, Pallas kernels, fused(): pl.pallas_call(kernel, out_shape=[pltpu.VMEM(o.shape, o.dtype) for o in o...  57.9 us

profile of v3, /device:TPU:1, one launch (start us, length us, event | category | flops | bytes accessed | tf_op | source)
XLA Modules:
  0.0 59.3 jit_solution(2620217923759874273)
XLA Ops:
  0.6 57.9 %shard_map.199 = (bf16[128,256]{1,0:T(8,128)(2,1)S(1)}, bf16[128,256]{1,0:T(8,128)(2,1)S(1)}, bf16[128,256]{1,0:T(8,128)(2,1)S(1)}, bf16[128,256]{1,0:T(8,128)(2...) custom-call(bf16[128,256]{1,0:T(8,128)(2,1)} %q1_ref.1, bf16[128,256]{1,0:T(8,128)(2,1)} %q2_ref.1, ...), custom_call_target="tpu_custom_call" | custom-call | tf_op jit(solution)/shard_map/pallas_call | solution.py:524
  58.5 0.8 %shard_map.200 = (bf16[128,256]{1,0:T(8,128)(2,1)}, bf16[128,256]{1,0:T(8,128)(2,1)}, bf16[128,256]{1,0:T(8,128)(2,1)}, bf16[128,256]{1,0:T(8,128)(2,1)}, bf16[128,512]{1,0:T(8,128)(2,1)}, /*index=5*/f32[4,128]{1,0:T(4,128)}) custom-call(bf16[128,256]{1,0:T(8,128)(2,1)S(1)} %get-tuple-element.12.refs_0_, bf16[128,256]{1,0:T(8,128)(2,1)S(1)} %get-tuple-element.13.refs_1_, ...), custom_call_target="tpu_custom_call" | custom-call | tf_op jit(solution)/shard_map/pallas_call | solution.py:537
